TPU v7x, 32 devices: a whole 2x2x4 slice. The times are simulated.
32 devices in a mesh: groups: 2 (over x), pts: 16 (over z, y, core).
Axes of the slice: x: 2, y: 2, z: 4, core: 2. Of those that a mesh axis runs over, the one named last changes fastest.
Arguments:
- points: bfloat16 [24576, 768], P(('groups', 'pts')), parts along dimension 0, may hold values from -6 to 6
- coverage: float32 [24576], P(('groups', 'pts')), parts along dimension 0, may hold values from 0 to 1.5
- candidates: bfloat16 [16384, 768], P(('groups', 'pts')), parts along dimension 0, may hold values from -0.21875 to 0.21875
- cand_mask: int32 [16384], P(('groups', 'pts')), parts along dimension 0, may hold values from 0 to 1, as said below
- send_block: int32 [32, 16], P(('groups', 'pts')), parts along dimension 0, may hold values from 0 to 3, as said below
- recv_src: int32 [32, 12], P(('groups', 'pts')), parts along dimension 0, may hold values from 0 to 15, as said below
- recv_block: int32 [32, 12], P(('groups', 'pts')), parts along dimension 0, may hold values from 0 to 3, as said below
- recv_live: int32 [32, 12], P(('groups', 'pts')), parts along dimension 0, may hold values from 0 to 1, as said below
Outputs:
- gains: float32 [16384], P(('groups', 'pts')), parts along dimension 0
There are 2 independent parts, one for each index of `groups`. A program takes and returns all parts, laid end to end along the dimension named above; each array names one. Nothing has to cross between parts.
Inputs may be any that keep to these rules, and one draw needn't show every extreme that they name: Point shards 2 k to 2 k + 1 hold all points of cluster k. Every candidate block belongs to one cluster; a cluster has at most 12 blocks, some cluster exactly 12, and no device owns two blocks of one cluster. Padding rows (cand_mask 0) lie only at the end of a cluster's last block, fewer than half of it. send_block[d, p] is d's local block of the cluster of shard p when d owns one (exactly when d appears among p's live receive entries), else 0. `recv_src`: the live entries of row d come first and name each block of shard d's cluster once, so each owner at most once; dead entries name d itself. On live entries recv_block[d, r] equals send_block[recv_src[d, r], d]; dead entries are 0. `recv_live`: row d has as many live entries as its cluster has blocks; the rows of some shard are all live.
All inputs are finite; a program needn't handle non-finite values.
Results may differ from a plain program's by a relative error of at most 0.0003.
Values may be sent and summed in bfloat16 or wider, within the bound.
A program may use at most 128 MiB of HBM per device.

v0:
```python
import jax
import jax.numpy as jnp
from jax import lax
from jax.sharding import PartitionSpec as P

BLK = 128


def clipped_sums(blocks, shard, levels):
    scores = lax.dot_general(
        blocks, shard, (((2,), (1,)), ((), ())), preferred_element_type=jnp.float32
    )
    return jnp.sum(jnp.maximum(scores - levels[None, None, :], 0.0), axis=2)


def on_device(points, coverage, candidates, cand_mask, send_block, recv_src, recv_block, recv_live):
    peers = lax.axis_size("pts")
    shard_rows, width = points.shape
    owned = candidates.shape[0] // BLK
    cand_blocks = candidates.reshape(owned, BLK, width)
    outgoing = jnp.take(cand_blocks, send_block[0], axis=0)
    sources = recv_src[0]
    living = recv_live[0].astype(jnp.float32)
    owners = (sources[:, None] == jnp.arange(peers, dtype=jnp.int32)[None, :]).astype(
        jnp.float32
    ) * living[:, None]

    def score_group(group):
        return clipped_sums(group, points, coverage)

    incoming = lax.all_to_all(outgoing, "pts", split_axis=0, concat_axis=0, tiled=True)
    items = incoming.shape[1]
    chosen = jnp.take(incoming, sources, axis=0)
    grouped = chosen.reshape(3, -1, items, width)
    partial_value = lax.map(score_group, grouped).reshape(-1, items)
    slot_gains = jnp.einsum("rp,rk->pk", owners, partial_value, precision=lax.Precision.HIGHEST)
    returned = lax.all_to_all(slot_gains, "pts", split_axis=0, concat_axis=0, tiled=True)
    placing = (send_block[0][:, None] == jnp.arange(owned, dtype=jnp.int32)[None, :]).astype(
        jnp.float32
    )
    totals = jnp.einsum("pb,pk->bk", placing, returned, precision=lax.Precision.HIGHEST)
    return totals.reshape(-1) * cand_mask.astype(jnp.float32) / shard_rows


def solution(mesh):
    return jax.shard_map(
        on_device,
        mesh=mesh,
        in_specs=(
            P(("groups", "pts"), None),
            P(("groups", "pts")),
            P(("groups", "pts"), None),
            P(("groups", "pts")),
            P(("groups", "pts"), None),
            P(("groups", "pts"), None),
            P(("groups", "pts"), None),
            P(("groups", "pts"), None),
        ),
        out_specs=P(("groups", "pts")),
        check_vma=False,
    )
```

profile of v0, /device:TPU:0, one launch (start us, length us, event | category | flops | bytes accessed | tf_op | source)
XLA Modules:
  0.0 109.1 jit_solution(15973549414584583682)
XLA Ops:
  0.0 0.0 copy-start
  0.0 0.7 fusion.12
  0.7 0.7 compare_and_fusion
  1.4 0.0 copy-done
  1.4 2.4 %gather_fusion = bf16[16,128,768]{2,1,0:T(8,128)(2,1)} fusion(bf16[4,128,768]{2,1,0:T(8,128)(2,1)S(1)} %bitcast.41, s32[1024]{0:T(1024)S(1)} %pad_clamp_fusion.1), kind=kCustom, calls=%fused_computation | custom fusion | bytes 6291520 | tf_op jit(solution)/shard_map/jit(_take)/gather | solution.py:21
  3.8 3.9 %broadcast_select_fusion = bf16[16,128,768]{2,1,0:T(8,128)(2,1)} fusion(bf16[16,128,768]{2,1,0:T(8,128)(2,1)} %gather_fusion, pred[16]{0:T(512)(128)(4,1)S(1)} %compare_and_fusion), kind=kLoop, calls=%fused_computation.8 | loop fusion | flops 1572864 | bytes 6291472 | tf_op jit(solution)/shard_map/jit(_take)/select_n | solution.py:21
  7.7 7.6 %all-to-all-start = ((bf16[16,128,768]{2,1,0:T(8,128)(2,1)}), bf16[16,128,768]{2,1,0:T(8,128)(2,1)}, u32[]{:S(2)}, u32[]{:S(2)}) async-start(bf16[16,128,768]{2,1,0:T(8,128)(2,1)} %broadcast_select_fusion), calls=%async_computation | async-start | bytes 6291456 | tf_op jit(solution)/shard_map/all_to_all | solution.py:31
  15.3 0.5 broadcast.95
  15.8 0.0 copy-done.4
  15.8 0.6 reduce.3
  16.4 0.1 eq.40
  16.5 0.0 copy-done.3
  16.6 58.2 %all-to-all-done = bf16[16,128,768]{2,1,0:T(8,128)(2,1)} async-done(((bf16[16,128,768]{2,1,0:T(8,128)(2,1)}), bf16[16,128,768]{2,1,0:T(8,128)(2,1)}, u32[]{:S(2)}, u32[]{:S(2)}) %all-to-all-start) | async-done | bytes 3145760 | tf_op jit(solution)/shard_map/all_to_all | solution.py:31
  74.7 2.6 %gather_fusion.1 = bf16[12,128,768]{2,1,0:T(8,128)(2,1)S(1)} fusion(bf16[16,128,768]{2,1,0:T(8,128)(2,1)} %all-to-all-done, s32[1024]{0:T(1024)S(1)} %pad_clamp_fusion), kind=kCustom, calls=%fused_computation.1 | custom fusion | bytes 4718640 | tf_op jit(solution)/shard_map/jit(_take)/gather | solution.py:33
  77.3 0.0 copy-start.1
  77.3 1.7 %broadcast_select_fusion.1 = bf16[3,4,128,768]{3,2,1,0:T(8,128)(2,1)} fusion(bf16[3,4,128,768]{3,2,1,0:T(8,128)(2,1)S(1)} %bitcast.42, pred[3,4]{1,0:T(4,128)(4,1)S(1)} %compare_and_fusion.1), kind=kLoop, calls=%fused_computation.9 | loop fusion | flops 1179648 | bytes 4718604 | tf_op jit(solution)/shard_map/jit(_take)/select_n | solution.py:33
  79.1 0.0 copy-done.1
  79.1 7.3 %while.10 = (s32[]{:T(128)}, f32[3,4,128]{2,1,0:T(4,128)S(1)}, bf16[3,4,128,768]{3,2,1,0:T(8,128)(2,1)}, bf16[768,768]{1,0:T(8,128)(2,1)}, f32[768]{0:T(1024)S(1)}, /*index=5*/s32[]{:T(128)}) while((s32[]{:T(128)}, f32[3,4,128]{2,1,0:T(4,128)S(1)}, bf16[3,4,128,768]{3,2,1,0:T(8,128)(2,1)}, bf16[768,768]{1,0:T(8,128)(2,1)}, f32[768]{0:T(1024)S(1)}, ...), condition=%wide.region_2.3_spmd, body=%wide.region_0.0_spmd.sunk | while | flops 605158912 | bytes 1975881 | solution.py:35
  79.1 2.4 %maximum_reduce_fusion.2 = f32[4,128]{1,0:T(4,128)S(1)} fusion(bf16[768,768]{1,0:T(8,128)(2,1)} %get-tuple-element.89, f32[768]{0:T(1024)S(1)} %get-tuple-element.90, bf16[3,4,128,768]{3,2,1,0:T(8,128)(2,1)} %get-tuple-element.88, s32[]{:T(128)} %get-tuple-element.80), kind=kOutput, calls=%fused_computation.2.clone.1 | convolution fusion | flops 605158912 | bytes 1971712 | tf_op jit(solution)/shard_map/while/body/eval_jaxpr/dot_general | solution.py:10
  81.5 2.4 %maximum_reduce_fusion.2 = f32[4,128]{1,0:T(4,128)S(1)} fusion(bf16[768,768]{1,0:T(8,128)(2,1)} %get-tuple-element.89, f32[768]{0:T(1024)S(1)} %get-tuple-element.90, bf16[3,4,128,768]{3,2,1,0:T(8,128)(2,1)} %get-tuple-element.88, s32[]{:T(128)} %get-tuple-element.80), kind=kOutput, calls=%fused_computation.2.clone.1 | convolution fusion | flops 605158912 | bytes 1971712 | tf_op jit(solution)/shard_map/while/body/eval_jaxpr/dot_general | solution.py:10
  84.0 2.4 %maximum_reduce_fusion.2 = f32[4,128]{1,0:T(4,128)S(1)} fusion(bf16[768,768]{1,0:T(8,128)(2,1)} %get-tuple-element.89, f32[768]{0:T(1024)S(1)} %get-tuple-element.90, bf16[3,4,128,768]{3,2,1,0:T(8,128)(2,1)} %get-tuple-element.88, s32[]{:T(128)} %get-tuple-element.80), kind=kOutput, calls=%fused_computation.2.clone.1 | convolution fusion | flops 605158912 | bytes 1971712 | tf_op jit(solution)/shard_map/while/body/eval_jaxpr/dot_general | solution.py:10
  86.4 0.3 fusion.6
  86.7 21.6 %all_to_all.17 = f32[16,1,128]{2,1,0:T(1,128)S(1)} all-to-all(f32[16,1,128]{2,1,0:T(1,128)S(1)} %bitcast.43), channel_id=1, replica_groups=mesh['groups'=2,'pts'=16] {'pts'}, dimensions={0} | all-to-all | bytes 16384 | tf_op jit(solution)/shard_map/all_to_all | solution.py:37
  108.3 0.8 fusion.5
  (16 shorter events, 0.1 us)
Async XLA Ops:
  0.0 1.4 %copy-start = (bf16[512,768]{1,0:T(8,128)(2,1)S(1)}, bf16[512,768]{1,0:T(8,128)(2,1)}, u32[]{:S(2)}) copy-start(bf16[512,768]{1,0:T(8,128)(2,1)} %param.12) | copy-start | bytes 2359300
  7.7 8.1 %copy-start.4 = (s32[1,12]{1,0:T(1,128)S(1)}, s32[1,12]{1,0:T(1,128)}, u32[]{:S(2)}) copy-start(s32[1,12]{1,0:T(1,128)} %param.15) | copy-start | bytes 148
  7.7 8.8 %copy-start.3 = (s32[1,12]{1,0:T(1,128)S(1)}, s32[1,12]{1,0:T(1,128)}, u32[]{:S(2)}) copy-start(s32[1,12]{1,0:T(1,128)} %param.16) | copy-start | bytes 148
  7.7 67.0 %all-to-all-start = ((bf16[16,128,768]{2,1,0:T(8,128)(2,1)}), bf16[16,128,768]{2,1,0:T(8,128)(2,1)}, u32[]{:S(2)}, u32[]{:S(2)}) async-start(bf16[16,128,768]{2,1,0:T(8,128)(2,1)} %broadcast_select_fusion), calls=%async_computation | async-start | bytes 6291456 | tf_op jit(solution)/shard_map/all_to_all | solution.py:31
  77.3 1.7 %copy-start.1 = (f32[768]{0:T(1024)S(1)}, f32[768]{0:T(1024)}, u32[]{:S(2)}) copy-start(f32[768]{0:T(1024)} %param.11) | copy-start | bytes 9220
  79.1 29.2 %copy-start.2 = (s32[512]{0:T(512)S(1)}, s32[512]{0:T(512)}, u32[]{:S(2)}) copy-start(s32[512]{0:T(512)} %param.13) | copy-start | bytes 6148
  79.1 29.2 %copy-start.5 = (s32[1,16]{1,0:T(1,128)S(1)}, s32[1,16]{1,0:T(1,128)}, u32[]{:S(2)}) copy-start(s32[1,16]{1,0:T(1,128)} %param.14) | copy-start | bytes 196
where the time goes:
time: 110 us; the launch traced here: 109 us
  waiting for transfers between devices  58.2 us (53%)
  blocking collectives  21.6 us (20%)
  matrix products  8.34 us (8%)
  other arithmetic  7.64 us (7%)
  starting transfers between devices  7.56 us (7%)
  local copies, waits for them, and re-layouts  5.65 us (5%)
    all_to_all x1, waiting for transfers between devices, on_device(): lax.all_to_all(outgoing, 'pts', split_axis=0, concat_axis=0, tiled=True)  58.2 us
    all_to_all x1, blocking collectives, on_device(): lax.all_to_all(slot_gains, 'pts', split_axis=0, concat_axis=0, tiled=True)  21.6 us
    all_to_all x1, starting transfers between devices, on_device(): lax.all_to_all(outgoing, 'pts', split_axis=0, concat_axis=0, tiled=True)  7.56 us
    dot_general x3, matrix products, clipped_sums(): lax.dot_general(blocks, shard, (((2,), (1,)), ((), ())), preferred_elemen...  7.24 us
    select_n x2, other arithmetic, on_device(): outgoing = jnp.take(cand_blocks, send_block[0], axis=0)  4.65 us
    gather x1, local copies, waits for them, and re-layouts, on_device(): chosen = jnp.take(incoming, sources, axis=0)  2.59 us
    gather x1, local copies, waits for them, and re-layouts, on_device(): outgoing = jnp.take(cand_blocks, send_block[0], axis=0)  2.41 us
  transfers between devices with their start and end apart: 1, of which 1 were waited for; matrix products, arithmetic and copies ran while one was open for 1% of the time, Pallas kernels for 0%

commit v1 on v0

v1 whole, which is shorter than its diff:
```python
import jax
import jax.numpy as jnp
from jax import lax
from jax.experimental import pallas as pl
from jax.experimental.pallas import tpu as pltpu
from jax.sharding import PartitionSpec as P

BLK = 128
LANES = 128
MESH = pl.DeviceIdType.MESH


def flipped(chip, step, chips):
    out = 0
    bit = 1
    while bit < chips:
        out = out + bit * ((chip // bit + step // bit) % 2)
        bit *= 2
    return out


def kernel(
    send_ref, src_ref, live_ref, points_ref, cov_ref, cand_ref, mask_ref, out_ref,
    inbox, stage, levels, living, part, ret,
    send_sem, recv_sem, give_sem, take_sem, back_sem, ret_sem,
):
    peers = ret.shape[0]
    chips = peers // 2
    owned = cand_ref.shape[0]
    shard_rows = points_ref.shape[0]
    me = lax.axis_index("pts")
    chip = me // 2
    core = me % 2
    sibling = chip * 2 + 1 - core

    barrier = pltpu.get_barrier_semaphore()

    def greet(s, _):
        pl.semaphore_signal(
            barrier, inc=1, device_id={"pts": (me + s) % peers}, device_id_type=MESH
        )
        return 0

    lax.fori_loop(1, peers, greet, 0)

    def pick(j, _):
        stage[j] = cand_ref[send_ref[0, 2 * j]]
        return 0

    lax.fori_loop(0, chips, pick, 0)

    def half(j, c):
        return inbox.at[j, pl.ds(pl.multiple_of(c * BLK, BLK), BLK), :]

    inbox[chip, pl.ds(pl.multiple_of(core * BLK, BLK), BLK), :] = cand_ref[send_ref[0, 2 * chip]]
    pl.semaphore_wait(barrier, peers - 1)

    def across(j, source):
        return pltpu.make_async_remote_copy(
            src_ref=stage.at[j],
            dst_ref=half(source, core),
            send_sem=send_sem.at[j],
            recv_sem=recv_sem.at[source],
            device_id={"pts": j * 2 + core},
            device_id_type=MESH,
        )

    def forward(j, c):
        return pltpu.make_async_remote_copy(
            src_ref=half(j, c),
            dst_ref=half(j, c),
            send_sem=give_sem.at[j],
            recv_sem=take_sem.at[j],
            device_id={"pts": sibling},
            device_id_type=MESH,
        )

    def give_back(owner, shard):
        return pltpu.make_async_remote_copy(
            src_ref=part.at[owner],
            dst_ref=ret.at[shard],
            send_sem=back_sem.at[owner],
            recv_sem=ret_sem.at[shard],
            device_id={"pts": owner},
            device_id_type=MESH,
        )

    def launch(t, _):
        across(flipped(chip, chips - t, chips), chip).start()
        return 0

    lax.fori_loop(1, chips, launch, 0)
    forward(chip, core).start()

    for i in range(shard_rows // LANES):
        row = cov_ref[pl.ds(i * LANES, LANES)].reshape(1, LANES)
        levels[pl.ds(i * LANES, LANES), :] = jnp.broadcast_to(row, (LANES, LANES)).T
    hits = (
        (lax.broadcasted_iota(jnp.int32, (peers, 1, src_ref.shape[1]), 0) == src_ref[...][None])
        & (live_ref[...][None] > 0)
    ).astype(jnp.float32)
    living[...] = jnp.broadcast_to(jnp.max(hits, axis=2, keepdims=True), living.shape)

    def score(j):
        forward(j, 1 - core).wait_recv()
        scores = lax.dot_general(
            points_ref[...], inbox[j], (((1,), (1,)), ((), ())),
            preferred_element_type=jnp.float32,
        )
        level = jnp.concatenate([levels[...], levels[...]], axis=1)
        sums = jnp.sum(jnp.maximum(scores - level, 0.0), axis=0, keepdims=True)
        part[2 * j] = sums[:, :BLK] * living[2 * j]
        part[2 * j + 1] = sums[:, BLK:] * living[2 * j + 1]

    def send_pair(j):
        give_back(2 * j, me).start()
        give_back(2 * j + 1, me).start()

    def arrive(j):
        across(chip, j).wait_recv()
        forward(j, core).start()

    arrive(flipped(chip, 1, chips))
    score(chip)
    ret[me] = part[me]
    give_back(sibling, me).start()

    def step(s, _):
        arrive(flipped(chip, s, chips))
        j = flipped(chip, s - 1, chips)
        score(j)
        send_pair(j)
        return 0

    lax.fori_loop(2, chips, step, 0)
    last = flipped(chip, chips - 1, chips)
    score(last)
    send_pair(last)

    def returned(s, _):
        give_back(me, (me + s) % peers).wait_recv()
        return 0

    lax.fori_loop(1, peers, returned, 0)

    def credit(p, total):
        slot = lax.broadcasted_iota(jnp.int32, (owned, BLK), 0)
        return total + jnp.where(slot == send_ref[0, p], ret[p], 0.0)

    total = lax.fori_loop(0, peers, credit, jnp.zeros((owned, BLK), jnp.float32))
    for b in range(owned):
        rows = pl.ds(b * BLK, BLK)
        out_ref[rows] = total[b] * mask_ref[rows].astype(jnp.float32) / shard_rows

    def drain_across(s, _):
        across(flipped(chip, s, chips), chip).wait_send()
        return 0

    lax.fori_loop(1, chips, drain_across, 0)

    def drain_forward(j, _):
        forward(j, core).wait_send()
        return 0

    lax.fori_loop(0, chips, drain_forward, 0)

    def drain_back(s, _):
        give_back((me + s) % peers, me).wait_send()
        return 0

    lax.fori_loop(1, peers, drain_back, 0)


def on_device(points, coverage, candidates, cand_mask, send_block, recv_src, recv_block, recv_live):
    peers = lax.axis_size("pts")
    chips = peers // 2
    rows, width = points.shape
    owned = candidates.shape[0] // BLK
    vmem = pl.BlockSpec(memory_space=pltpu.VMEM)
    block_bytes = BLK * width * 2
    need = (3 * chips + owned) * block_bytes + rows * width * 2 + rows * LANES * 4
    return pl.pallas_call(
        kernel,
        out_shape=jax.ShapeDtypeStruct((owned * BLK,), jnp.float32),
        in_specs=[pl.BlockSpec(memory_space=pltpu.SMEM)] + [vmem] * 6,
        out_specs=vmem,
        scratch_shapes=[
            pltpu.VMEM((chips, 2 * BLK, width), jnp.bfloat16),
            pltpu.VMEM((chips, BLK, width), jnp.bfloat16),
            pltpu.VMEM((rows, LANES), jnp.float32),
            pltpu.VMEM((peers, 1, LANES), jnp.float32),
            pltpu.VMEM((peers, 1, LANES), jnp.float32),
            pltpu.VMEM((peers, 1, LANES), jnp.float32),
            pltpu.SemaphoreType.DMA((chips,)),
            pltpu.SemaphoreType.DMA((chips,)),
            pltpu.SemaphoreType.DMA((chips,)),
            pltpu.SemaphoreType.DMA((chips,)),
            pltpu.SemaphoreType.DMA((peers,)),
            pltpu.SemaphoreType.DMA((peers,)),
        ],
        compiler_params=pltpu.CompilerParams(
            collective_id=0, has_side_effects=True, vmem_limit_bytes=need + (12 << 20)
        ),
    )(
        send_block, recv_src, recv_live, points, coverage,
        candidates.reshape(owned, BLK, width), cand_mask,
    )


def solution(mesh):
    return jax.shard_map(
        on_device,
        mesh=mesh,
        in_specs=(
            P(("groups", "pts"), None),
            P(("groups", "pts")),
            P(("groups", "pts"), None),
            P(("groups", "pts")),
            P(("groups", "pts"), None),
            P(("groups", "pts"), None),
            P(("groups", "pts"), None),
            P(("groups", "pts"), None),
        ),
        out_specs=P(("groups", "pts")),
        check_vma=False,
    )
```

time: 110 us -> 59.4 us (0.54)
  waiting for transfers between devices: 58.2 us -> 0 us
  Pallas kernels: 0 us -> 52.8 us
  blocking collectives: 21.6 us -> 0 us
  matrix products: 8.34 us -> 0 us
  other arithmetic: 7.64 us -> 0 us
  starting transfers between devices: 7.56 us -> 0 us
    all_to_all x1 -> x0, waiting for transfers between devices: 58.2 us -> none  [on_device(): lax.all_to_all(outgoing, 'pts', split_axis=0, concat_axis=0, tiled=True)]
    pallas_call x0 -> x1, Pallas kernels: none -> 52.8 us  [on_device(): pl.pallas_call(kernel, out_shape=jax.ShapeDtypeStruct((owned * BLK,), jnp...]
    all_to_all x1 -> x0, blocking collectives: 21.6 us -> none  [on_device(): lax.all_to_all(slot_gains, 'pts', split_axis=0, concat_axis=0, tiled=True)]
    dot_general x5 -> x0, matrix products: 8.34 us -> none  [the longest x3 7.24 us: clipped_sums(): lax.dot_general(blocks, shard, (((2,), (1,)), ((), ())), preferred_elemen...]
    all_to_all x1 -> x0, starting transfers between devices: 7.56 us -> none  [on_device(): lax.all_to_all(outgoing, 'pts', split_axis=0, concat_axis=0, tiled=True)]
    select_n x4 -> x0, other arithmetic: 6.36 us -> none  [the longest x2 4.65 us: on_device(): outgoing = jnp.take(cand_blocks, send_block[0], axis=0)]
    unnamed x13 -> x15, local copies, waits for them, and re-layouts: 0.53 us -> 6.31 us
    gather x2 -> x0, local copies, waits for them, and re-layouts: 5 us -> none  [the longest x1 2.59 us: on_device(): chosen = jnp.take(incoming, sources, axis=0)]
  transfers between devices with their start and end apart: 1 -> 0, of which waited for: 1 -> 0; matrix products, arithmetic and copies ran while one was open for 1% -> 0% of each run, Pallas kernels for 0% -> 0%
where the time goes in v1:
time: 59.4 us; the launch traced here: 59.1 us
  Pallas kernels  52.8 us (89%)
  local copies, waits for them, and re-layouts  6.31 us (11%)
    pallas_call x1, Pallas kernels, on_device(): pl.pallas_call(kernel, out_shape=jax.ShapeDtypeStruct((owned * BLK,), jnp...  52.8 us
    unnamed x15, local copies, waits for them, and re-layouts  6.31 us

profile of v1, /device:TPU:0, one launch (start us, length us, event | category | flops | bytes accessed | tf_op | source)
XLA Modules:
  0.0 59.1 jit_solution(7310507420864651793)
XLA Ops:
  0.0 0.0 copy-start
  0.0 1.3 %copy-done = bf16[768,768]{1,0:T(8,128)(2,1)S(1)} copy-done((bf16[768,768]{1,0:T(8,128)(2,1)S(1)}, bf16[768,768]{1,0:T(8,128)(2,1)}, u32[]{:S(2)}) %copy-start) | copy-done | bytes 1179672
  1.3 0.0 copy-start.1
  1.3 1.1 %copy-done.1 = bf16[512,768]{1,0:T(8,128)(2,1)S(1)} copy-done((bf16[512,768]{1,0:T(8,128)(2,1)S(1)}, bf16[512,768]{1,0:T(8,128)(2,1)}, u32[]{:S(2)}) %copy-start.1) | copy-done | bytes 786456
  2.4 0.0 copy-start.2
  2.4 0.7 %copy-done.2 = f32[768]{0:T(1024)S(1)} copy-done((f32[768]{0:T(1024)S(1)}, f32[768]{0:T(1024)}, u32[]{:S(2)}) %copy-start.2) | copy-done | bytes 3096
  3.1 0.0 copy-start.3
  3.1 0.7 %copy-done.3 = s32[512]{0:T(512)S(1)} copy-done((s32[512]{0:T(512)S(1)}, s32[512]{0:T(512)}, u32[]{:S(2)}) %copy-start.3) | copy-done | bytes 2072
  3.8 0.0 copy-start.4
  3.8 0.7 %copy-done.4 = s32[1,16]{1,0:T(1,128)S(1)} copy-done((s32[1,16]{1,0:T(1,128)S(1)}, s32[1,16]{1,0:T(1,128)}, u32[]{:S(2)}) %copy-start.4) | copy-done | bytes 88
  4.4 0.0 copy-start.5
  4.4 0.7 %copy-done.5 = s32[1,12]{1,0:T(1,128)S(1)} copy-done((s32[1,12]{1,0:T(1,128)S(1)}, s32[1,12]{1,0:T(1,128)}, u32[]{:S(2)}) %copy-start.5) | copy-done | bytes 72
  5.1 0.0 copy-start.6
  5.1 0.7 %copy-done.6 = s32[1,12]{1,0:T(1,128)S(1)} copy-done((s32[1,12]{1,0:T(1,128)S(1)}, s32[1,12]{1,0:T(1,128)}, u32[]{:S(2)}) %copy-start.6) | copy-done | bytes 72
  5.7 52.8 %shard_map.73 = f32[512]{0:T(512)S(1)} custom-call(s32[1,16]{1,0:T(1,128)S(1)} %copy-done.4, s32[1,12]{1,0:T(1,128)S(1)} %copy-done.5, s32[1,12]{1,0:T(1,128)S(1)} %copy-done.6, bf16[768,768]{1,0:T(8,128)(2,1)S(1)} %copy-done, f32[768]{0:T(1024)S(1)} %copy-done.2, bf16[4,128,768]{2,1,0:T(8,128)(2,1)S(1)} %bitcast.1, s32[512]{0:T(512)S(1)} %copy-done.3), custom_call_target="tpu_custom_call" | custom-call | tf_op jit(solution)/shard_map/pallas_call | solution.py:182
  58.5 0.6 copy.9
Async XLA Ops:
  0.0 1.3 %copy-start = (bf16[768,768]{1,0:T(8,128)(2,1)S(1)}, bf16[768,768]{1,0:T(8,128)(2,1)}, u32[]{:S(2)}) copy-start(bf16[768,768]{1,0:T(8,128)(2,1)} %points_ref.1) | copy-start | bytes 3538948
  1.3 1.1 %copy-start.1 = (bf16[512,768]{1,0:T(8,128)(2,1)S(1)}, bf16[512,768]{1,0:T(8,128)(2,1)}, u32[]{:S(2)}) copy-start(bf16[512,768]{1,0:T(8,128)(2,1)} %param.10) | copy-start | bytes 2359300
  2.4 0.7 %copy-start.2 = (f32[768]{0:T(1024)S(1)}, f32[768]{0:T(1024)}, u32[]{:S(2)}) copy-start(f32[768]{0:T(1024)} %cov_ref.1) | copy-start | bytes 9220
  3.1 0.7 %copy-start.3 = (s32[512]{0:T(512)S(1)}, s32[512]{0:T(512)}, u32[]{:S(2)}) copy-start(s32[512]{0:T(512)} %mask_ref.1) | copy-start | bytes 6148
  3.8 0.7 %copy-start.4 = (s32[1,16]{1,0:T(1,128)S(1)}, s32[1,16]{1,0:T(1,128)}, u32[]{:S(2)}) copy-start(s32[1,16]{1,0:T(1,128)} %send_ref.1) | copy-start | bytes 196
  4.4 0.7 %copy-start.5 = (s32[1,12]{1,0:T(1,128)S(1)}, s32[1,12]{1,0:T(1,128)}, u32[]{:S(2)}) copy-start(s32[1,12]{1,0:T(1,128)} %src_ref.1) | copy-start | bytes 148
  5.1 0.7 %copy-start.6 = (s32[1,12]{1,0:T(1,128)S(1)}, s32[1,12]{1,0:T(1,128)}, u32[]{:S(2)}) copy-start(s32[1,12]{1,0:T(1,128)} %live_ref.1) | copy-start | bytes 148

commit v2 on v1

--- a/solution.py
+++ b/solution.py
@@ -20,8 +20,8 @@
 
 
 def kernel(
-    send_ref, src_ref, live_ref, points_ref, cov_ref, cand_ref, mask_ref, out_ref,
-    inbox, stage, levels, living, part, ret,
+    send_hbm, src_hbm, live_hbm, points_hbm, cov_hbm, cand_hbm, mask_hbm, out_ref,
+    send_ref, src_ref, live_ref, points_ref, cov_ref, cand_ref, mask_ref, fetch_sem, inbox, stage, levels, living, part, ret,
     send_sem, recv_sem, give_sem, take_sem, back_sem, ret_sem,
 ):
     peers = ret.shape[0]
@@ -33,6 +33,15 @@
     core = me % 2
     sibling = chip * 2 + 1 - core
 
+    pairs = (
+        (send_hbm, send_ref), (cand_hbm, cand_ref), (points_hbm, points_ref), (cov_hbm, cov_ref),
+        (src_hbm, src_ref), (live_hbm, live_ref), (mask_hbm, mask_ref),
+    )
+    fetches = [
+        pltpu.make_async_copy(far, near, fetch_sem.at[i]) for i, (far, near) in enumerate(pairs)
+    ]
+    for fetch in fetches:
+        fetch.start()
     barrier = pltpu.get_barrier_semaphore()
 
     def greet(s, _):
@@ -42,6 +51,9 @@
         return 0
 
     lax.fori_loop(1, peers, greet, 0)
+
+    fetches[0].wait()
+    fetches[1].wait()
 
     def pick(j, _):
         stage[j] = cand_ref[send_ref[0, 2 * j]]
@@ -86,12 +98,14 @@
         )
 
     def launch(t, _):
-        across(flipped(chip, chips - t, chips), chip).start()
+        across(flipped(chip, t, chips), chip).start()
         return 0
 
     lax.fori_loop(1, chips, launch, 0)
     forward(chip, core).start()
 
+    for fetch in fetches[2:]:
+        fetch.wait()
     for i in range(shard_rows // LANES):
         row = cov_ref[pl.ds(i * LANES, LANES)].reshape(1, LANES)
         levels[pl.ds(i * LANES, LANES), :] = jnp.broadcast_to(row, (LANES, LANES)).T
@@ -182,9 +196,17 @@
     return pl.pallas_call(
         kernel,
         out_shape=jax.ShapeDtypeStruct((owned * BLK,), jnp.float32),
-        in_specs=[pl.BlockSpec(memory_space=pltpu.SMEM)] + [vmem] * 6,
+        in_specs=[pl.BlockSpec(memory_space=pltpu.HBM)] * 7,
         out_specs=vmem,
         scratch_shapes=[
+            pltpu.SMEM(send_block.shape, jnp.int32),
+            pltpu.VMEM(recv_src.shape, jnp.int32),
+            pltpu.VMEM(recv_live.shape, jnp.int32),
+            pltpu.VMEM(points.shape, points.dtype),
+            pltpu.VMEM(coverage.shape, jnp.float32),
+            pltpu.VMEM((owned, BLK, width), candidates.dtype),
+            pltpu.VMEM(cand_mask.shape, jnp.int32),
+            pltpu.SemaphoreType.DMA((7,)),
             pltpu.VMEM((chips, 2 * BLK, width), jnp.bfloat16),
             pltpu.VMEM((chips, BLK, width), jnp.bfloat16),
             pltpu.VMEM((rows, LANES), jnp.float32),

time: 59.4 us -> 52.2 us (0.88)
  the two profiles are of different devices: /device:TPU:0 before, /device:TPU:8 now
where the time goes in v2:
time: 52.2 us; the launch traced here: 52 us
  Pallas kernels  45.6 us (87%)
  local copies, waits for them, and re-layouts  6.31 us (12%)
    pallas_call x1, Pallas kernels, on_device(): pl.pallas_call(kernel, out_shape=jax.ShapeDtypeStruct((owned * BLK,), jnp...  45.6 us
    unnamed x15, local copies, waits for them, and re-layouts  6.31 us

profile of v2, /device:TPU:8, one launch (start us, length us, event | category | flops | bytes accessed | tf_op | source)
XLA Modules:
  0.0 52.0 jit_solution(5831310228280425191)
XLA Ops:
  0.0 0.0 copy-start
  0.0 1.3 %copy-done = bf16[768,768]{1,0:T(8,128)(2,1)S(1)} copy-done((bf16[768,768]{1,0:T(8,128)(2,1)S(1)}, bf16[768,768]{1,0:T(8,128)(2,1)}, u32[]{:S(2)}) %copy-start) | copy-done | bytes 1179672
  1.3 0.0 copy-start.1
  1.3 1.1 %copy-done.1 = bf16[512,768]{1,0:T(8,128)(2,1)S(1)} copy-done((bf16[512,768]{1,0:T(8,128)(2,1)S(1)}, bf16[512,768]{1,0:T(8,128)(2,1)}, u32[]{:S(2)}) %copy-start.1) | copy-done | bytes 786456
  2.4 0.0 copy-start.2
  2.4 0.7 %copy-done.2 = f32[768]{0:T(1024)S(1)} copy-done((f32[768]{0:T(1024)S(1)}, f32[768]{0:T(1024)}, u32[]{:S(2)}) %copy-start.2) | copy-done | bytes 3096
  3.1 0.0 copy-start.3
  3.1 0.7 %copy-done.3 = s32[512]{0:T(512)S(1)} copy-done((s32[512]{0:T(512)S(1)}, s32[512]{0:T(512)}, u32[]{:S(2)}) %copy-start.3) | copy-done | bytes 2072
  3.8 0.0 copy-start.4
  3.8 0.7 %copy-done.4 = s32[1,16]{1,0:T(1,128)S(1)} copy-done((s32[1,16]{1,0:T(1,128)S(1)}, s32[1,16]{1,0:T(1,128)}, u32[]{:S(2)}) %copy-start.4) | copy-done | bytes 88
  4.4 0.0 copy-start.5
  4.4 0.7 %copy-done.5 = s32[1,12]{1,0:T(1,128)S(1)} copy-done((s32[1,12]{1,0:T(1,128)S(1)}, s32[1,12]{1,0:T(1,128)}, u32[]{:S(2)}) %copy-start.5) | copy-done | bytes 72
  5.1 0.0 copy-start.6
  5.1 0.7 %copy-done.6 = s32[1,12]{1,0:T(1,128)S(1)} copy-done((s32[1,12]{1,0:T(1,128)S(1)}, s32[1,12]{1,0:T(1,128)}, u32[]{:S(2)}) %copy-start.6) | copy-done | bytes 72
  5.7 45.6 %shard_map.73 = f32[512]{0:T(512)S(1)} custom-call(s32[1,16]{1,0:T(1,128)S(1)} %copy-done.4, s32[1,12]{1,0:T(1,128)S(1)} %copy-done.5, s32[1,12]{1,0:T(1,128)S(1)} %copy-done.6, bf16[768,768]{1,0:T(8,128)(2,1)S(1)} %copy-done, f32[768]{0:T(1024)S(1)} %copy-done.2, bf16[4,128,768]{2,1,0:T(8,128)(2,1)S(1)} %bitcast.1, s32[512]{0:T(512)S(1)} %copy-done.3), custom_call_target="tpu_custom_call" | custom-call | tf_op jit(solution)/shard_map/pallas_call | solution.py:196
  51.4 0.6 %copy.9 = f32[512]{0:T(512)} copy(f32[512]{0:T(512)S(1)} %shard_map.73) | data formatting | bytes 4096
Async XLA Ops:
  0.0 1.3 %copy-start = (bf16[768,768]{1,0:T(8,128)(2,1)S(1)}, bf16[768,768]{1,0:T(8,128)(2,1)}, u32[]{:S(2)}) copy-start(bf16[768,768]{1,0:T(8,128)(2,1)} %points_hbm.1) | copy-start | bytes 3538948
  1.3 1.1 %copy-start.1 = (bf16[512,768]{1,0:T(8,128)(2,1)S(1)}, bf16[512,768]{1,0:T(8,128)(2,1)}, u32[]{:S(2)}) copy-start(bf16[512,768]{1,0:T(8,128)(2,1)} %param.10) | copy-start | bytes 2359300
  2.4 0.7 %copy-start.2 = (f32[768]{0:T(1024)S(1)}, f32[768]{0:T(1024)}, u32[]{:S(2)}) copy-start(f32[768]{0:T(1024)} %cov_hbm.1) | copy-start | bytes 9220
  3.1 0.7 %copy-start.3 = (s32[512]{0:T(512)S(1)}, s32[512]{0:T(512)}, u32[]{:S(2)}) copy-start(s32[512]{0:T(512)} %mask_hbm.1) | copy-start | bytes 6148
  3.8 0.7 %copy-start.4 = (s32[1,16]{1,0:T(1,128)S(1)}, s32[1,16]{1,0:T(1,128)}, u32[]{:S(2)}) copy-start(s32[1,16]{1,0:T(1,128)} %send_hbm.1) | copy-start | bytes 196
  4.4 0.7 %copy-start.5 = (s32[1,12]{1,0:T(1,128)S(1)}, s32[1,12]{1,0:T(1,128)}, u32[]{:S(2)}) copy-start(s32[1,12]{1,0:T(1,128)} %src_hbm.1) | copy-start | bytes 148
  5.1 0.7 %copy-start.6 = (s32[1,12]{1,0:T(1,128)S(1)}, s32[1,12]{1,0:T(1,128)}, u32[]{:S(2)}) copy-start(s32[1,12]{1,0:T(1,128)} %live_hbm.1) | copy-start | bytes 148

commit v3 on v2

--- a/solution.py
+++ b/solution.py
@@ -40,7 +40,7 @@
     fetches = [
         pltpu.make_async_copy(far, near, fetch_sem.at[i]) for i, (far, near) in enumerate(pairs)
     ]
-    for fetch in fetches:
+    for fetch in fetches[:2]:
         fetch.start()
     barrier = pltpu.get_barrier_semaphore()
 
@@ -54,6 +54,8 @@
 
     fetches[0].wait()
     fetches[1].wait()
+    for fetch in fetches[2:]:
+        fetch.start()
 
     def pick(j, _):
         stage[j] = cand_ref[send_ref[0, 2 * j]]
@@ -126,30 +128,43 @@
         part[2 * j] = sums[:, :BLK] * living[2 * j]
         part[2 * j + 1] = sums[:, BLK:] * living[2 * j + 1]
 
-    def send_pair(j):
-        give_back(2 * j, me).start()
-        give_back(2 * j + 1, me).start()
-
     def arrive(j):
         across(chip, j).wait_recv()
         forward(j, core).start()
 
-    arrive(flipped(chip, 1, chips))
-    score(chip)
-    ret[me] = part[me]
-    give_back(sibling, me).start()
-
     def step(s, _):
-        arrive(flipped(chip, s, chips))
+        @pl.when(s < chips)
+        def _():
+            arrive(flipped(chip, s, chips))
+
         j = flipped(chip, s - 1, chips)
         score(j)
-        send_pair(j)
-        return 0
-
-    lax.fori_loop(2, chips, step, 0)
-    last = flipped(chip, chips - 1, chips)
-    score(last)
-    send_pair(last)
+
+        @pl.when(s == 1)
+        def _():
+            ret[me] = part[me]
+            give_back(sibling, me).start()
+
+        @pl.when(s > 1)
+        def _():
+            give_back(2 * j, me).start()
+            give_back(2 * j + 1, me).start()
+
+        return 0
+
+    lax.fori_loop(1, chips + 1, step, 0)
+
+    def drain_across(s, _):
+        across(flipped(chip, s, chips), chip).wait_send()
+        return 0
+
+    lax.fori_loop(1, chips, drain_across, 0)
+
+    def drain_forward(j, _):
+        forward(j, core).wait_send()
+        return 0
+
+    lax.fori_loop(0, chips, drain_forward, 0)
 
     def returned(s, _):
         give_back(me, (me + s) % peers).wait_recv()
@@ -165,18 +180,6 @@
     for b in range(owned):
         rows = pl.ds(b * BLK, BLK)
         out_ref[rows] = total[b] * mask_ref[rows].astype(jnp.float32) / shard_rows
-
-    def drain_across(s, _):
-        across(flipped(chip, s, chips), chip).wait_send()
-        return 0
-
-    lax.fori_loop(1, chips, drain_across, 0)
-
-    def drain_forward(j, _):
-        forward(j, core).wait_send()
-        return 0
-
-    lax.fori_loop(0, chips, drain_forward, 0)
 
     def drain_back(s, _):
         give_back((me + s) % peers, me).wait_send()
@@ -221,7 +224,7 @@
             pltpu.SemaphoreType.DMA((peers,)),
         ],
         compiler_params=pltpu.CompilerParams(
-            collective_id=0, has_side_effects=True, vmem_limit_bytes=need + (12 << 20)
+            collective_id=0, has_side_effects=True, vmem_limit_bytes=max(need + (12 << 20), 60 << 20)
         ),
     )(
         send_block, recv_src, recv_live, points, coverage,

time: 52.2 us -> 47.1 us (0.902)
  local copies, waits for them, and re-layouts: 6.31 us -> 1.26 us
    unnamed x15 -> x1, local copies, waits for them, and re-layouts: 6.31 us -> 1.26 us
where the time goes in v3:
time: 47.1 us; the launch traced here: 46.9 us
  Pallas kernels  45.6 us (97%)
  local copies, waits for them, and re-layouts  1.26 us (3%)
    pallas_call x1, Pallas kernels, on_device(): pl.pallas_call(kernel, out_shape=jax.ShapeDtypeStruct((owned * BLK,), jnp...  45.6 us
    unnamed x1, local copies, waits for them, and re-layouts  1.26 us

profile of v3, /device:TPU:8, one launch (start us, length us, event | category | flops | bytes accessed | tf_op | source)
XLA Modules:
  0.0 46.9 jit_solution(6171546453641685354)
XLA Ops:
  0.0 45.6 %shard_map.73 = f32[512]{0:T(512)} custom-call(s32[1,16]{1,0:T(1,128)} %send_hbm.1, s32[1,12]{1,0:T(1,128)} %src_hbm.1, s32[1,12]{1,0:T(1,128)} %live_hbm.1, bf16[768,768]{1,0:T(8,128)(2,1)} %points_hbm.1, f32[768]{0:T(1024)} %cov_hbm.1, bf16[4,128,768]{2,1,0:T(8,128)(2,1)} %bitcast.1, s32[512]{0:T(512)} %mask_hbm.1), custom_call_target="tpu_custom_call" | custom-call | tf_op jit(solution)/shard_map/pallas_call | solution.py:199
  45.6 1.3 %copy.9 = f32[512]{0:T(512)} copy(f32[512]{0:T(512)} %shard_map.73) | data formatting | bytes 4096

commit v4 on v3

--- a/solution.py
+++ b/solution.py
@@ -166,17 +166,21 @@
 
     lax.fori_loop(0, chips, drain_forward, 0)
 
-    def returned(s, _):
-        give_back(me, (me + s) % peers).wait_recv()
-        return 0
-
-    lax.fori_loop(1, peers, returned, 0)
+    slot = lax.broadcasted_iota(jnp.int32, (owned, BLK), 0)
 
     def credit(p, total):
-        slot = lax.broadcasted_iota(jnp.int32, (owned, BLK), 0)
         return total + jnp.where(slot == send_ref[0, p], ret[p], 0.0)
 
-    total = lax.fori_loop(0, peers, credit, jnp.zeros((owned, BLK), jnp.float32))
+    def returned(s, total):
+        j = flipped(chip, s, chips)
+        for p in (2 * j, 2 * j + 1):
+            give_back(me, p).wait_recv()
+            total = credit(p, total)
+        return total
+
+    give_back(me, sibling).wait_recv()
+    total = credit(sibling, credit(me, jnp.zeros((owned, BLK), jnp.float32)))
+    total = lax.fori_loop(1, chips, returned, total)
     for b in range(owned):
         rows = pl.ds(b * BLK, BLK)
         out_ref[rows] = total[b] * mask_ref[rows].astype(jnp.float32) / shard_rows
@@ -224,11 +228,16 @@
             pltpu.SemaphoreType.DMA((peers,)),
         ],
         compiler_params=pltpu.CompilerParams(
-            collective_id=0, has_side_effects=True, vmem_limit_bytes=max(need + (12 << 20), 60 << 20)
+            collective_id=0, has_side_effects=True, vmem_limit_bytes=need + (12 << 20)
         ),
     )(
-        send_block, recv_src, recv_live, points, coverage,
-        candidates.reshape(owned, BLK, width), cand_mask,
+        *(
+            pltpu.with_memory_space_constraint(x, pltpu.HBM)
+            for x in (
+                send_block, recv_src, recv_live, points, coverage,
+                candidates.reshape(owned, BLK, width), cand_mask,
+            )
+        )
     )
 
 

time: 47.1 us -> 45.7 us (0.970)
  Pallas kernels: 45.6 us -> 44.9 us
  local copies, waits for them, and re-layouts: 1.26 us -> 0.58 us
    pallas_call x1, Pallas kernels: 45.6 us -> 44.9 us  [on_device(): pl.pallas_call(kernel, out_shape=jax.ShapeDtypeStruct((owned * BLK,), jnp...]
    unnamed x1, local copies, waits for them, and re-layouts: 1.26 us -> 0.58 us
where the time goes in v4:
time: 45.7 us; the launch traced here: 45.5 us
  Pallas kernels  44.9 us (98%)
  local copies, waits for them, and re-layouts  0.58 us (1%)
    pallas_call x1, Pallas kernels, on_device(): pl.pallas_call(kernel, out_shape=jax.ShapeDtypeStruct((owned * BLK,), jnp...  44.9 us

profile of v4, /device:TPU:8, one launch (start us, length us, event | category | flops | bytes accessed | tf_op | source)
XLA Modules:
  0.0 45.5 jit_solution(16170577243316635804)
XLA Ops:
  0.0 44.9 %shard_map.73 = f32[512]{0:T(512)S(1)} custom-call(s32[1,16]{1,0:T(1,128)} %send_hbm.1, s32[1,12]{1,0:T(1,128)} %src_hbm.1, s32[1,12]{1,0:T(1,128)} %live_hbm.1, bf16[768,768]{1,0:T(8,128)(2,1)} %points_hbm.1, f32[768]{0:T(1024)} %cov_hbm.1, bf16[4,128,768]{2,1,0:T(8,128)(2,1)} %bitcast.1, s32[512]{0:T(512)} %mask_hbm.1), custom_call_target="tpu_custom_call" | custom-call | tf_op jit(solution)/shard_map/pallas_call | solution.py:203
  44.9 0.6 %copy.9 = f32[512]{0:T(512)} copy(f32[512]{0:T(512)S(1)} %shard_map.73) | data formatting | bytes 4096
